TPU v7x, 512 devices: a whole 4x4x16 slice. The times are simulated.
512 devices in a mesh: dp: 2 (over core), fsdp: 32 (over y, z_lo), tensor: 8 (over z_hi, x).
Axes of the slice: x: 4, y: 4, z: 16 (z_hi: 2, z_lo: 8; z = z_hi * 8 + z_lo), core: 2. Of those that a mesh axis runs over, the one named last changes fastest.
Arguments:
- tokens: bfloat16 [16384, 4096], P(('dp', 'fsdp', 'tensor')), may hold values from -40 to 40
- norm_gain: float32 [4096], replicated, may hold values from 0.5 to 1.5
- tile_values: bfloat16 [512, 128, 128], P(('fsdp', 'tensor')), may hold values from -0.25 to 0.25
- tile_rows: int32 [8, 64], P('tensor'), may hold values from 0 to 31, as said below
- tile_cols: int32 [8, 64], P('tensor'), may hold values from 0 to 13
- tile_counts: int32 [8, 32], P('tensor'), may hold values from 0 to 2, as said below
- grad_out: bfloat16 [16384, 14336], P(('dp', 'fsdp'), 'tensor'), may hold values from -3 to 3
Outputs:
- mixed: bfloat16 [16384, 14336], P(('dp', 'fsdp'), 'tensor')
- grad_x: bfloat16 [16384, 4096], P(('dp', 'fsdp', 'tensor'))
- grad_gain: float32 [4096], replicated
- grad_tiles: float32 [512, 128, 128], P(('fsdp', 'tensor'))
Inputs may be any that keep to these rules, and one draw needn't show every extreme that they name: `tile_counts`: for each tensor index the counts over the 32 fsdp shards sum to 56, and some shard holds exactly 2. `tile_rows`: within one tensor index the (row, column) pairs of held slots are all different.
All inputs are finite; a program needn't handle non-finite values.
Results may differ from a plain program's by a relative error of at most 0.013.
Values may be sent and summed in bfloat16 or wider, within the bound.
A program may use at most 128 MiB of HBM per device.

v0:
```python
import jax
import jax.numpy as jnp
from jax import lax
from jax.sharding import PartitionSpec as P


def tile_forward(group_rows, values, rows_list, cols_list, col_tiles):
    tile_size = values.shape[1]
    blocks = group_rows.reshape(group_rows.shape[0], -1, tile_size)
    picked = jnp.take(blocks, rows_list, axis=1)
    product = jnp.einsum("tsk,skn->tsn", picked, values, preferred_element_type=jnp.float32)
    placed = (
        jnp.zeros((group_rows.shape[0], col_tiles, tile_size), jnp.float32)
        .at[:, cols_list]
        .add(product)
    )
    return placed.reshape(group_rows.shape[0], col_tiles * tile_size)


def tile_backward(grad_rows, values, rows_list, cols_list, row_tiles):
    tile_size = values.shape[1]
    blocks = grad_rows.reshape(grad_rows.shape[0], -1, tile_size)
    picked = jnp.take(blocks, cols_list, axis=1)
    product = jnp.einsum("tsn,skn->tsk", picked, values, preferred_element_type=jnp.float32)
    placed = (
        jnp.zeros((grad_rows.shape[0], row_tiles, tile_size), jnp.float32)
        .at[:, rows_list]
        .add(product)
    )
    return placed.reshape(grad_rows.shape[0], row_tiles * tile_size)


def per_device(tokens, norm_gain, tile_values, tile_rows, tile_cols, tile_counts, grad_out):
    tile_size = tile_values.shape[1]
    slot_cap = tile_values.shape[0]
    row_tiles = tokens.shape[1] // tile_size
    col_tiles = grad_out.shape[1] // tile_size
    rows_list = tile_rows[0]
    cols_list = tile_cols[0]
    shard_counts = tile_counts[0]
    held_all = (jnp.arange(slot_cap)[None, :] < shard_counts[:, None]).reshape(-1)
    own_held = jnp.arange(slot_cap) < shard_counts[lax.axis_index("fsdp")]
    local_float = tokens.astype(jnp.float32)
    inv_rms = lax.rsqrt(jnp.mean(local_float * local_float, axis=1, keepdims=True) + 1e-05)
    scaled = local_float * inv_rms
    normed = (scaled * norm_gain).astype(jnp.bfloat16)
    group_rows = lax.all_gather(normed, "tensor", axis=0, tiled=True)
    gathered = lax.all_gather(tile_values, "fsdp", axis=0, tiled=True)
    kept_values = jnp.where(held_all[:, None, None], gathered, jnp.zeros_like(gathered))
    outputs = tile_forward(group_rows, kept_values, rows_list, cols_list, col_tiles)
    mixed = outputs.astype(jnp.bfloat16)
    input_grad = lax.psum_scatter(
        tile_backward(grad_out, kept_values, rows_list, cols_list, row_tiles).astype(jnp.bfloat16),
        "tensor",
        scatter_dimension=0,
        tiled=True,
    ).astype(jnp.float32)
    x_blocks = group_rows.reshape(group_rows.shape[0], row_tiles, tile_size)
    g_blocks = grad_out.reshape(grad_out.shape[0], col_tiles, tile_size)
    picked_x = jnp.take(x_blocks, rows_list, axis=1)
    picked_g = jnp.take(g_blocks, cols_list, axis=1)
    grad_shard = lax.psum_scatter(
        jnp.einsum("tsk,tsn->skn", picked_x, picked_g, preferred_element_type=jnp.float32),
        "fsdp",
        scatter_dimension=0,
        tiled=True,
    )
    grad_shard = jnp.where(own_held[:, None, None], grad_shard, jnp.zeros_like(grad_shard))
    grad_tiles = lax.psum(grad_shard, "dp")
    gain_part = jnp.sum(input_grad * scaled, axis=0)
    grad_gain = lax.psum(gain_part, ("dp", "fsdp", "tensor"))
    hidden_grad = input_grad * norm_gain
    grad_x = (
        inv_rms * (hidden_grad - scaled * jnp.mean(hidden_grad * scaled, axis=1, keepdims=True))
    ).astype(jnp.bfloat16)
    return (mixed, grad_x, grad_gain, grad_tiles)


def solution(mesh):
    placed = (
        P(("dp", "fsdp", "tensor"), None),
        P(),
        P(("fsdp", "tensor"), None, None),
        P("tensor", None),
        P("tensor", None),
        P("tensor", None),
        P(("dp", "fsdp"), "tensor"),
    )
    return jax.shard_map(
        per_device,
        mesh=mesh,
        in_specs=placed,
        out_specs=(
            P(("dp", "fsdp"), "tensor"),
            P(("dp", "fsdp", "tensor"), None),
            P(),
            P(("fsdp", "tensor"), None, None),
        ),
        check_vma=False,
    )
```

profile of v0, /device:TPU:1, one launch (start us, length us, event | category | flops | bytes accessed | tf_op | source)
XLA Modules:
  0.0 848.5 jit_solution(9026113694259479338)
XLA Ops:
  7.9 1.5 copy.32
  11.6 3.1 gather_fusion.1
  14.7 207.7 %all-gather.3.cloned.1.call-done = bf16[64,128,128]{2,1,0:T(8,128)(2,1)} async-done(((bf16[2,128,128]{2,1,0:T(8,128)(2,1)}), bf16[64,128,128]{2,1,0:T(8,128)(2,1)}) %all-gather.3.cloned.1.call-update) | async-done | bytes 2097168 | tf_op jit(solution)/shard_map/all_gather | solution.py:48
  222.3 7.4 fusion.2
  229.8 2.4 broadcast_in_dim.57
  232.2 19.4 %scatter_fusion.1 = f32[256,32,128]{2,0,1:T(8,128)} fusion(f32[256,32,128]{2,0,1:T(8,128)} %broadcast_in_dim.57, s32[64]{0:T(128)S(1)} %fusion.18, f32[64,256,128]{2,1,0:T(8,128)} %fusion.2), kind=kCustom, calls=%fused_computation.3 | custom fusion | flops 2097152 | bytes 25166080 | tf_op jit(solution)/shard_map/scatter-add | solution.py:28
  251.6 2.5 convert_element_type.28
  254.1 2.9 copy.34
  257.0 4.1 copy.39
  261.4 162.8 %reduce-scatter.7.cloned.1.call-done = bf16[32,4096]{1,0:T(8,128)(2,1)} async-done(((bf16[256,4096]{1,0:T(8,128)(2,1)}), bf16[32,4096]{1,0:T(8,128)(2,1)}) %reduce-scatter.7.cloned.1.call-update) | async-done | bytes 262160 | tf_op jit(solution)/shard_map/reduce_scatter | solution.py:52
  425.5 1.9 fusion.12
  427.6 109.9 %all-gather.5.cloned.1.call-done = bf16[256,4096]{1,0:T(8,128)(2,1)} async-done(((bf16[32,4096]{1,0:T(8,128)(2,1)}), bf16[256,4096]{1,0:T(8,128)(2,1)}) %all-gather.5.cloned.1.call-update) | async-done | bytes 2097168 | tf_op jit(solution)/shard_map/all_gather | solution.py:47
  537.5 4.1 copy.29
  541.6 3.2 copy.30
  544.8 3.0 gather_fusion
  547.8 7.0 fusion
  556.7 103.2 %psum.14 = f32[4096]{0:T(1024)} all-reduce(f32[4096]{0:T(1024)S(1)} %get-tuple-element.18), channel_id=1, replica_groups=mesh['dp'=2,'fsdp'=32,'tensor'=8] {'dp','fsdp','tensor'}, use_global_device_ids=true, to_apply=%region_6.9 | all-reduce | flops 4096 | bytes 32768 | tf_op jit(solution)/shard_map/psum | solution.py:71
  659.9 119.5 %reduce-scatter.5.cloned.1.call-done = f32[2,128,128]{2,1,0:T(8,128)} async-done(((f32[64,128,128]{2,1,0:T(8,128)}), f32[2,128,128]{2,1,0:T(8,128)}) %reduce-scatter.5.cloned.1.call-update) | async-done | bytes 131088 | tf_op jit(solution)/shard_map/reduce_scatter | solution.py:62
  779.5 1.6 broadcast_select_fusion.9
  781.1 6.7 fusion.5
  788.0 12.4 %scatter_fusion = f32[256,14,128]{2,0,1:T(8,128)S(1)} fusion(f32[256,14,128]{2,0,1:T(8,128)S(1)} %broadcast_in_dim.54, s32[64]{0:T(128)S(1)} %fusion.17, f32[64,256,128]{2,1,0:T(8,128)} %fusion.5), kind=kCustom, calls=%fused_computation.2 | custom fusion | flops 2097152 | bytes 25166080 | tf_op jit(solution)/shard_map/scatter-add | solution.py:15
  801.2 1.4 copy.37
  802.5 37.8 %all-reduce.2.cloned.1.call-done = f32[2,128,128]{2,1,0:T(8,128)} async-done(((f32[2,128,128]{2,1,0:T(8,128)}), f32[2,128,128]{2,1,0:T(8,128)}) %all-reduce.2.cloned.1.call-update) | async-done | bytes 131088 | tf_op jit(solution)/shard_map/psum | solution.py:69
  840.4 1.6 copy.44
  (41 shorter events, 7.2 us)
Async XLA Ops:
  7.2 215.2 %all-gather.3.cloned.1.call-start = ((), (), s32[]{:S(2)}) async-start(), calls=%async_computation.2 | async-start | bytes 2162688 | tf_op jit(solution)/shard_map/all_gather | solution.py:48
  7.9 416.4 %reduce-scatter.7.cloned.1.call-start = ((), (), s32[]{:S(2)}) async-start(), calls=%async_computation.6 | async-start | bytes 2359296 | tf_op jit(solution)/shard_map/reduce_scatter | solution.py:52
  11.6 3.1 copy-start.4
  11.6 3.1 copy-start.5
  257.0 4.2 copy-start.1
  257.0 167.2 %copy-start.2 = (f32[4096]{0:T(1024)S(1)}, f32[4096]{0:T(1024)}, u32[]{:S(2)}) copy-start(f32[4096]{0:T(1024)} %param.12) | copy-start | bytes 49156
  261.2 276.3 %all-gather.5.cloned.1.call-start = ((), (), s32[]{:S(2)}) async-start(), calls=%async_computation.3 | async-start | bytes 2359296 | tf_op jit(solution)/shard_map/all_gather | solution.py:47
  427.5 352.0 %reduce-scatter.5.cloned.1.call-start = ((), (), s32[]{:S(2)}) async-start(), calls=%async_computation.4 | async-start | bytes 4325376 | tf_op jit(solution)/shard_map/reduce_scatter | solution.py:62
  554.8 0.7 copy-start.3
  554.8 226.3 %copy-start = (bf16[64,128,128]{2,1,0:T(8,128)(2,1)S(1)}, bf16[64,128,128]{2,1,0:T(8,128)(2,1)}, u32[]{:S(2)}) copy-start(bf16[64,128,128]{2,1,0:T(8,128)(2,1)} %all-gather.3.cloned.1.call-done) | copy-start | bytes 6291460
  554.9 285.5 %all-reduce.2.cloned.1.call-start = ((), (), s32[]{:S(2)}) async-start(), calls=%async_computation.5 | async-start | bytes 262144 | tf_op jit(solution)/shard_map/psum | solution.py:69
Sparse Core Ops, SparseCore 0:
  10.1 212.2 all-gather.2
  261.3 162.8 reduce-scatter.6
  428.5 108.9 all-gather.4
  555.0 224.4 reduce-scatter.4
  783.0 57.3 all-reduce.1
where the time goes:
time: 849 us; the launch traced here: 848 us
  waiting for transfers between devices  639 us (75%)
  blocking collectives  103 us (12%)
  other arithmetic  41.6 us (5%)
  local copies, waits for them, and re-layouts  29.9 us (4%)
  matrix products  21.2 us (2%)
  between operations  13.9 us (2%)
    all_gather x1, waiting for transfers between devices, per_device(): gathered = lax.all_gather(tile_values, 'fsdp', axis=0, tiled=True)  208 us
    reduce_scatter x1, waiting for transfers between devices, per_device(): lax.psum_scatter(tile_backward(grad_out, kept_values, rows_list, cols_lis...  163 us
    reduce_scatter x1, waiting for transfers between devices, per_device(): lax.psum_scatter(jnp.einsum('tsk,tsn->skn', picked_x, picked_g, preferred...  120 us
    all_gather x1, waiting for transfers between devices, per_device(): group_rows = lax.all_gather(normed, 'tensor', axis=0, tiled=True)  110 us
    psum x1, blocking collectives, per_device(): grad_gain = lax.psum(gain_part, ('dp', 'fsdp', 'tensor'))  103 us
    psum x1, waiting for transfers between devices, per_device(): grad_tiles = lax.psum(grad_shard, 'dp')  37.8 us
    scatter-add x1, other arithmetic, tile_backward(): placed = jnp.zeros((grad_rows.shape[0], row_tiles, tile_size), jnp.float3...  19.4 us
  transfers between devices with their start and end apart: 5, of which 5 were waited for; matrix products, arithmetic and copies ran while one was open for 3% of the time, Pallas kernels for 0%

commit v1 on v0

--- a/solution.py
+++ b/solution.py
@@ -1,7 +1,19 @@
+import functools
 import jax
 import jax.numpy as jnp
 from jax import lax
 from jax.sharding import PartitionSpec as P
+
+
+def touch_positions_now(block_here, comm_axis, peer_axis):
+    for s in (comm_axis, peer_axis):
+        block_here = lax.psum(block_here, axis_name=s)
+    return block_here
+
+
+try_all_corner = functools.partial(
+    touch_positions_now, comm_axis="dp", peer_axis=("fsdp", "tensor")
+)
 
 
 def tile_forward(group_rows, values, rows_list, cols_list, col_tiles):
@@ -68,7 +80,7 @@
     grad_shard = jnp.where(own_held[:, None, None], grad_shard, jnp.zeros_like(grad_shard))
     grad_tiles = lax.psum(grad_shard, "dp")
     gain_part = jnp.sum(input_grad * scaled, axis=0)
-    grad_gain = lax.psum(gain_part, ("dp", "fsdp", "tensor"))
+    grad_gain = try_all_corner(gain_part)
     hidden_grad = input_grad * norm_gain
     grad_x = (
         inv_rms * (hidden_grad - scaled * jnp.mean(hidden_grad * scaled, axis=1, keepdims=True))

time: 849 us -> 2670 us (3.14)
  blocking collectives: 103 us -> 1830 us
  waiting for transfers between devices: 639 us -> 736 us
    psum x1 -> x2, blocking collectives: 103 us -> 1830 us  [touch_positions_now(): block_here = lax.psum(block_here, axis_name=s)]
    psum x1, waiting for transfers between devices: 37.8 us -> 255 us  [per_device(): grad_tiles = lax.psum(grad_shard, 'dp')]
    reduce_scatter x1, waiting for transfers between devices: 120 us -> 0.01 us  [per_device(): lax.psum_scatter(jnp.einsum('tsk,tsn->skn', picked_x, picked_g, preferred...]
  transfers between devices with their start and end apart: 5 -> 5, of which waited for: 5 -> 4; matrix products, arithmetic and copies ran while one was open for 3% -> 1% of each run, Pallas kernels for 0% -> 0%
where the time goes in v1:
time: 2670 us
  blocking collectives  1830 us (69%)
  waiting for transfers between devices  736 us (28%)
  other arithmetic  41.6 us (2%)
  local copies, waits for them, and re-layouts  29.9 us (1%)
    psum x2, blocking collectives, touch_positions_now(): block_here = lax.psum(block_here, axis_name=s)  1830 us
    psum x1, waiting for transfers between devices, per_device(): grad_tiles = lax.psum(grad_shard, 'dp')  255 us
    all_gather x1, waiting for transfers between devices, per_device(): gathered = lax.all_gather(tile_values, 'fsdp', axis=0, tiled=True)  208 us
    reduce_scatter x1, waiting for transfers between devices, per_device(): lax.psum_scatter(tile_backward(grad_out, kept_values, rows_list, cols_lis...  163 us
    all_gather x1, waiting for transfers between devices, per_device(): group_rows = lax.all_gather(normed, 'tensor', axis=0, tiled=True)  110 us
  transfers between devices with their start and end apart: 5, of which 4 were waited for; matrix products, arithmetic and copies ran while one was open for 1% of the time, Pallas kernels for 0%

profile of v1, /device:TPU:1, one launch (start us, length us, event | category | flops | bytes accessed | tf_op | source)
XLA Modules:
  0.0 2668.8 jit_solution(11433064209790548050)
XLA Ops:
  7.9 1.5 copy.32
  11.6 3.1 gather_fusion.1
  14.7 207.7 %all-gather.3.cloned.1.call-done = bf16[64,128,128]{2,1,0:T(8,128)(2,1)} async-done(((bf16[2,128,128]{2,1,0:T(8,128)(2,1)}), bf16[64,128,128]{2,1,0:T(8,128)(2,1)}) %all-gather.3.cloned.1.call-update) | async-done | bytes 2097168 | tf_op jit(solution)/shard_map/all_gather | solution.py:60
  222.3 7.4 fusion.2
  229.8 2.4 broadcast_in_dim.57
  232.2 19.4 scatter_fusion.1
  251.6 2.5 convert_element_type.28
  254.1 2.9 copy.34
  257.0 4.1 copy.39
  261.4 163.2 %reduce-scatter.7.cloned.1.call-done = bf16[32,4096]{1,0:T(8,128)(2,1)} async-done(((bf16[256,4096]{1,0:T(8,128)(2,1)}), bf16[32,4096]{1,0:T(8,128)(2,1)}) %reduce-scatter.7.cloned.1.call-update) | async-done | bytes 262160 | tf_op jit(solution)/shard_map/reduce_scatter | solution.py:64
  425.9 1.9 fusion.12
  428.0 109.9 %all-gather.5.cloned.1.call-done = bf16[256,4096]{1,0:T(8,128)(2,1)} async-done(((bf16[32,4096]{1,0:T(8,128)(2,1)}), bf16[256,4096]{1,0:T(8,128)(2,1)}) %all-gather.5.cloned.1.call-update) | async-done | bytes 2097168 | tf_op jit(solution)/shard_map/all_gather | solution.py:59
  537.8 4.1 copy.29
  541.9 3.2 copy.30
  545.1 3.0 gather_fusion
  548.2 7.0 fusion
  557.1 5.4 psum.21
  562.5 1820.2 %psum.22 = f32[4096]{0:T(1024)} all-reduce(f32[4096]{0:T(1024)S(1)} %psum.21), channel_id=1, replica_groups=mesh['dp'=2,'fsdp'=32,'tensor'=8] {'fsdp','tensor'}, use_global_device_ids=true, to_apply=%region_7.10 | all-reduce | flops 4096 | bytes 32768 | tf_op jit(solution)/shard_map/psum | solution.py:10
  2382.7 1.6 broadcast_select_fusion.9
  2384.4 6.7 fusion.5
  2391.3 12.4 scatter_fusion
  2404.4 1.4 copy.37
  2405.8 254.9 %all-reduce.2.cloned.1.call-done = f32[2,128,128]{2,1,0:T(8,128)} async-done(((f32[2,128,128]{2,1,0:T(8,128)}), f32[2,128,128]{2,1,0:T(8,128)}) %all-reduce.2.cloned.1.call-update) | async-done | bytes 131088 | tf_op jit(solution)/shard_map/psum | solution.py:81
  2660.7 1.6 copy.44
  (42 shorter events, 7.2 us)
Async XLA Ops:
  7.2 215.2 %all-gather.3.cloned.1.call-start = ((), (), s32[]{:S(2)}) async-start(), calls=%async_computation.2 | async-start | bytes 2162688 | tf_op jit(solution)/shard_map/all_gather | solution.py:60
  7.9 416.7 %reduce-scatter.7.cloned.1.call-start = ((), (), s32[]{:S(2)}) async-start(), calls=%async_computation.6 | async-start | bytes 2359296 | tf_op jit(solution)/shard_map/reduce_scatter | solution.py:64
  11.6 3.1 copy-start.4
  11.6 3.1 copy-start.5
  257.0 4.2 copy-start.1
  257.0 167.6 %copy-start.2 = (f32[4096]{0:T(1024)S(1)}, f32[4096]{0:T(1024)}, u32[]{:S(2)}) copy-start(f32[4096]{0:T(1024)} %param.12) | copy-start | bytes 49156
  261.2 276.6 %all-gather.5.cloned.1.call-start = ((), (), s32[]{:S(2)}) async-start(), calls=%async_computation.3 | async-start | bytes 2359296 | tf_op jit(solution)/shard_map/all_gather | solution.py:59
  427.9 1954.8 %reduce-scatter.5.cloned.1.call-start = ((), (), s32[]{:S(2)}) async-start(), calls=%async_computation.4 | async-start | bytes 4325376 | tf_op jit(solution)/shard_map/reduce_scatter | solution.py:74
  555.2 0.7 copy-start.3
  555.2 1829.2 %copy-start = (bf16[64,128,128]{2,1,0:T(8,128)(2,1)S(1)}, bf16[64,128,128]{2,1,0:T(8,128)(2,1)}, u32[]{:S(2)}) copy-start(bf16[64,128,128]{2,1,0:T(8,128)(2,1)} %all-gather.3.cloned.1.call-done) | copy-start | bytes 6291460
  555.2 2105.5 %all-reduce.2.cloned.1.call-start = ((), (), s32[]{:S(2)}) async-start(), calls=%async_computation.5 | async-start | bytes 262144 | tf_op jit(solution)/shard_map/psum | solution.py:81
Sparse Core Ops, SparseCore 0:
  10.1 212.2 all-gather.2
  261.3 163.2 reduce-scatter.6
  428.9 108.8 all-gather.4
  555.3 224.8 reduce-scatter.4
  2384.5 276.1 all-reduce.1
